TPU v7x, 512 devices: a whole 4x8x8 slice. The times are simulated.
512 devices in a mesh: patch: 128 (over z, y, core), mp: 4 (over x).
Axes of the slice: x: 4, y: 8, z: 8, core: 2. Of those that a mesh axis runs over, the one named last changes fastest.
Arguments:
- points: bfloat16 [65536, 256], P(('patch', 'mp')), may hold values from -6 to 6
- patch_counts: int32 [128], replicated, may hold values from 256 to 512, as said below
- to_hilbert: int32 [65536], P('patch'), may hold values from 0 to 65535, as said below
- from_hilbert: int32 [65536], P('patch'), may hold values from 0 to 65535, as said below
- cotangent: bfloat16 [65536, 256], P(('patch', 'mp')), may hold values from -0.0625 to 0.0625
- gain_mixer: float32 [2, 256], replicated, may hold values from 0.5 to 1.5
- query_weight: bfloat16 [2, 256, 256], replicated, may hold values from -0.375 to 0.375
- key_weight: bfloat16 [2, 256, 256], replicated, may hold values from -0.375 to 0.375
- value_weight: bfloat16 [2, 256, 256], replicated, may hold values from -0.375 to 0.375
- out_weight: bfloat16 [2, 256, 256], replicated, may hold values from -0.375 to 0.375
- gain_feed: float32 [2, 256], replicated, may hold values from 0.5 to 1.5
- up_weight: bfloat16 [2, 256, 1024], replicated, may hold values from -0.375 to 0.375
- down_weight: bfloat16 [2, 1024, 256], replicated, may hold values from -0.1875 to 0.1875
Outputs:
- hilbert_out: bfloat16 [65536, 256], P(('patch', 'mp'))
- grad_gain_mixer: float32 [2, 256], replicated
- grad_query: float32 [2, 256, 256], P(None, 'mp')
- grad_key: float32 [2, 256, 256], P(None, 'mp')
- grad_value: float32 [2, 256, 256], P(None, 'mp')
- grad_out: float32 [2, 256, 256], P(None, 'mp')
- grad_gain_feed: float32 [2, 256], replicated
- grad_up: float32 [2, 256, 1024], P(None, 'mp')
- grad_down: float32 [2, 1024, 256], P(None, 'mp')
Inputs may be any that keep to these rules, and one draw needn't show every extreme that they name: z-ordered patch i holds points in its first patch_counts[i] rows and padding in the rest. A permutation of the rows: z-ordered row r becomes Hilbert row to_hilbert[r]; of the 512 rows of one aligned block, at most 6 land in any one aligned block of 512 rows, and some pair of blocks reaches 6. `from_hilbert`: the inverse permutation of to_hilbert.
All inputs are finite; a program needn't handle non-finite values.
Results may differ from a plain program's by a relative error of at most 0.034.
Values may be sent and summed in bfloat16 or wider, within the bound.
No kernel may reach another device: no remote copies, remote signals or barrier semaphores. Data moves between devices by JAX's collectives and lax.ppermute only.
A program may use at most 64 MiB of HBM per device.

v0:
```python
import functools

import jax
import jax.numpy as jnp
from jax import lax
from jax.experimental import pallas as pl
from jax.experimental.pallas import tpu as pltpu
from jax.sharding import PartitionSpec as P

HEADS = 16
PATCH = 512
HEAD_DIM = 16
WIDTH = 256
HIDDEN = 1024
SLOTS = 6
PIECES = 1
VALUE_SCALE = 1024.0
ALLOWED = -0.0078125
LANES = 128
WEIGHT_ROWS = 768
HALF_ROWS = WEIGHT_ROWS + 16
GAIN_ROWS = 4
CHUNK_ROWS = 24 + GAIN_ROWS

EPSILON = 1e-05
GELU_SCALE = 0.7978845608028654
GELU_CUBIC = 0.044715

BF = jnp.bfloat16
F32 = jnp.float32


def dot(left, right, left_dim=1, right_dim=0):
    return lax.dot_general(
        left, right, (((left_dim,), (right_dim,)), ((), ())), preferred_element_type=F32
    )


def norm_rows(values, gain_row):
    widened = values.astype(F32)
    centered = widened - jnp.mean(widened, axis=1, keepdims=True)
    inverse = lax.rsqrt(jnp.mean(centered * centered, axis=1, keepdims=True) + EPSILON)
    normed = centered * inverse
    return normed, inverse, (normed * gain_row).astype(BF)


def norm_back(grad_scaled, normed, inverse, gain_row):
    grad_normed = grad_scaled * gain_row
    centered = grad_normed - jnp.mean(grad_normed, axis=1, keepdims=True)
    return inverse * (centered - normed * jnp.mean(grad_normed * normed, axis=1, keepdims=True))


def gelu(pre):
    tangent = jnp.tanh(GELU_SCALE * (pre + GELU_CUBIC * (pre * pre * pre)))
    return 0.5 * pre * (1.0 + tangent)


def gelu_pair(pre):
    squared = pre * pre
    tangent = jnp.tanh(GELU_SCALE * (pre + GELU_CUBIC * (squared * pre)))
    half = 0.5 * (1.0 + tangent)
    slopes = half + 0.5 * pre * (1.0 - tangent * tangent) * (
        GELU_SCALE + GELU_SCALE * 3.0 * GELU_CUBIC * squared
    )
    return pre * half, slopes


def flip(values):
    return values.astype(F32).T.astype(BF)


def head_rows(head):
    return slice(head * HEAD_DIM, (head + 1) * HEAD_DIM)


def fill_bias(live_column, bias_ref):
    keys = lax.broadcasted_iota(jnp.int32, (PATCH, PATCH), 0)
    queries = lax.broadcasted_iota(jnp.int32, (PATCH, PATCH), 1)
    allowed = (live_column > 0) | (keys == queries)
    bias_ref[...] = jnp.where(allowed, ALLOWED, -1e30)


def attend(query, key, value, s, after_head=None):
    s.query_t[...] = (query.astype(F32) * HEAD_DIM ** (-0.5)).T.astype(BF)
    s.value_t[...] = (value.astype(F32) * (1.0 / VALUE_SCALE)).T.astype(BF)

    for head in range(HEADS):
        rows = head_rows(head)
        weights = jnp.exp(dot(key[:, rows], s.query_t[rows, :]) + s.bias[...])
        inverse = 1.0 / jnp.sum(weights, axis=0, keepdims=True)
        s.inverse_sum[head] = inverse
        lowered = weights.astype(BF)
        s.weights[head] = lowered
        if after_head is not None:
            after_head(head)
        mixed = dot(s.value_t[rows, :], lowered)
        s.heads_t[rows, :] = (mixed * (inverse * VALUE_SCALE)).astype(BF)


def attend_back(key, value, grad_heads, s):
    s.key_t[...] = flip(key)
    s.grad_heads_t[...] = flip(grad_heads)
    query_t, heads_t, inverse_sum = s.query_t, s.heads_t, s.inverse_sum

    for head in range(HEADS):
        rows = head_rows(head)
        query_rows = query_t[rows, :]
        grad_rows = s.grad_heads_t[rows, :]
        probability = s.kept_weights(head).astype(F32) * inverse_sum[head]
        grad_wide = grad_rows.astype(F32) * HEAD_DIM ** (-0.5)
        inner = jnp.sum(grad_wide * heads_t[rows, :].astype(F32), axis=0, keepdims=True)
        grad_prob = dot(value[:, rows], grad_wide.astype(BF))
        grad_score = (probability * (grad_prob - inner)).astype(BF)
        s.grad_value_t[rows, :] = dot(grad_rows, probability.astype(BF), 1, 1).astype(BF)
        s.grad_query_t[rows, :] = dot(s.key_t[rows, :], grad_score).astype(BF)
        s.grad_key_t[rows, :] = (
            dot(query_rows, grad_score, 1, 1) * HEAD_DIM**0.5
        ).astype(BF)


def feed_forward(middle, up_weight, gain_feed):
    normed_m, inverse_m, scaled_m = norm_rows(middle, gain_feed)
    return normed_m, inverse_m, scaled_m, dot(scaled_m, up_weight)


def backward(part, core, grad_rows, x, middle, key, value, w, s, halves, want_grad_in):
    def put(first_row, grad):
        rows = slice(first_row, first_row + grad.shape[0])
        low, high = grad[:, :LANES], grad[:, LANES:]
        halves[0][rows, :] = jnp.where(core == 0, low, high).astype(halves[0].dtype)
        halves[1][rows, :] = jnp.where(core == 0, high, low).astype(halves[1].dtype)

    normed_m, inverse_m, scaled_m, pre = feed_forward(middle, w.up[...], w.gain_feed)
    activated, slopes = gelu_pair(pre)
    s.hidden[...] = activated.astype(BF)
    s.turned[...] = flip(scaled_m)
    quarter = pl.ds(pl.multiple_of(part * (WIDTH // 4), WIDTH // 4), WIDTH // 4)
    hidden_part = s.hidden[:, pl.ds(pl.multiple_of(part * WIDTH, WIDTH), WIDTH)]
    put(512, dot(hidden_part, grad_rows, 0, 0))
    grad_pre = (dot(grad_rows, w.down[...], 1, 1) * slopes).astype(BF)
    up_grad = dot(s.turned[quarter, :], grad_pre)
    for piece in range(4):
        put(256 + 64 * piece, up_grad[:, WIDTH * piece : WIDTH * (piece + 1)])
    grad_scaled_m = dot(grad_pre, w.up[...], 1, 1)
    feed_gain = jnp.sum(grad_scaled_m * normed_m, axis=0, keepdims=True)
    grad_middle = (
        grad_rows.astype(F32)
        + norm_back(grad_scaled_m, normed_m, inverse_m, w.gain_feed)
    ).astype(BF)
    put(192, dot(s.heads_t[quarter, :], grad_middle))
    grad_heads = dot(grad_middle, w.out[...], 1, 1).astype(BF)
    attend_back(key[...], value[...], grad_heads, s)
    normed_a, inverse_a, scaled_a = norm_rows(x[...].reshape(PATCH, WIDTH), w.gain_mixer)
    s.turned[...] = flip(scaled_a)
    scaled_part = s.turned[quarter, :]
    put(0, dot(scaled_part, s.grad_query_t[...], 1, 1))
    put(64, dot(scaled_part, s.grad_key_t[...], 1, 1))
    put(128, dot(scaled_part, s.grad_value_t[...], 1, 1))
    grad_scaled_a = (
        dot(w.query[...], s.grad_query_t[...])
        + dot(w.key[...], s.grad_key_t[...])
        + dot(w.value[...], s.grad_value_t[...])
    ).T
    mixer_gain = jnp.sum(grad_scaled_a * normed_a, axis=0, keepdims=True)
    gains = jnp.concatenate([mixer_gain, feed_gain, jnp.zeros((14, WIDTH), F32)], axis=0)
    put(WEIGHT_ROWS, gains)
    if not want_grad_in:
        return None
    return (
        grad_middle.astype(F32) + norm_back(grad_scaled_a, normed_a, inverse_a, w.gain_mixer)
    ).astype(BF)


class Inputs:
    def __init__(self, names, sources, buffers, sems, block, early):
        self.block, self.copies = block, {}
        self.buffers = dict(zip(names, buffers, strict=True))
        for place, (name, source) in enumerate(zip(names, sources, strict=True)):
            self.copies[name] = pltpu.make_async_copy(source, self.buffers[name], sems.at[place])
        self.rest = list(self.copies.values())[early:]
        for copy in list(self.copies.values())[:early]:
            copy.start()

    def wait(self, *names):
        for name in names:
            if name in self.copies:
                self.copies.pop(name).wait()

    def start_rest(self):
        for copy in self.rest:
            copy.start()
        self.rest = []

    def __getattr__(self, name):
        if name not in self.__dict__.get("buffers", ()):
            raise AttributeError(name)
        self.wait(name)
        if name in GAINS:
            return self.buffers[name][self.block : self.block + 1, :]
        return self.buffers[name]


class Scratch:
    def __init__(self, names, refs, inputs=None):
        self.inputs = inputs
        for name, ref in zip(names, refs, strict=True):
            setattr(self, name, ref)

    def __getattr__(self, name):
        return getattr(self.__dict__["inputs"], name)

    def kept_weights(self, head):
        if self.inputs is None:
            return self.weights[head]
        piece, place = divmod(head, HEADS // PIECES)
        return getattr(self.inputs, f"weights{piece}")[place]


def as_column(row):
    wide = jnp.broadcast_to(row.astype(F32), (8, row.shape[1]))
    return wide.T[:, :1].astype(jnp.int32)


GAINS = ("gain_mixer", "gain_feed")
WEIGHTS = ("gain_mixer", "query", "key", "value", "out", "gain_feed", "up", "down")
FORWARD_SCRATCH = (
    ("query_t", (WIDTH, PATCH), BF),
    ("value_t", (WIDTH, PATCH), BF),
    ("bias", (PATCH, PATCH), F32),
    ("weights", (HEADS, PATCH, PATCH), BF),
    ("inverse_sum", (HEADS, 1, PATCH), F32),
    ("heads_t", (WIDTH, PATCH), BF),
)
BACKWARD_SCRATCH = (
    ("key_t", (WIDTH, PATCH), BF),
    ("grad_heads_t", (WIDTH, PATCH), BF),
    ("grad_query_t", (WIDTH, PATCH), BF),
    ("grad_key_t", (WIDTH, PATCH), BF),
    ("grad_value_t", (WIDTH, PATCH), BF),
    ("turned", (WIDTH, PATCH), BF),
    ("hidden", (PATCH, HIDDEN), BF),
)


SCRATCH = {name: (shape, dtype) for name, shape, dtype in FORWARD_SCRATCH + BACKWARD_SCRATCH}
VMEM_BYTES = 58 * 1024 * 1024


def project(scaled, w):
    query = dot(scaled, w.query[...]).astype(BF)
    key = dot(scaled, w.key[...]).astype(BF)
    value = dot(scaled, w.value[...]).astype(BF)
    return query, key, value


def forward(x, live_column, w, s, after_head=None):
    fill_bias(live_column, s.bias)
    normed, inverse, scaled = norm_rows(x, w.gain_mixer)
    query, key, value = project(scaled, w)
    w.start_rest()
    attend(query, key, value, s, after_head)
    heads_out = s.heads_t[...].astype(F32).T.astype(BF)
    middle = (x.astype(F32) + dot(heads_out, w.out[...])).astype(BF)
    return key, value, middle


def own_live(count):
    return (lax.broadcasted_iota(jnp.int32, (PATCH, 1), 0) < count).astype(jnp.int32)


def block_of(rows):
    return lax.shift_right_logical(rows, PATCH.bit_length() - 1)


def places_of(targets, ranking):
    owners = block_of(targets)
    same = block_of(as_column(targets)) == owners
    ahead = same & (as_column(ranking) < ranking)
    return owners * SLOTS + jnp.sum(ahead.astype(F32), axis=0, keepdims=True).astype(jnp.int32)


def moved_live(sources, counts):
    column = as_column(sources)
    patches = lax.broadcasted_iota(jnp.int32, (PATCH, counts.shape[1]), 1)
    chosen = jnp.where(patches == block_of(column), counts.astype(F32), 0.0)
    count = jnp.sum(chosen, axis=1, keepdims=True).astype(jnp.int32)
    return ((column & (PATCH - 1)) < count).astype(jnp.int32)


def pack(rows, places, pairs_ref, packed_ref):
    slots = packed_ref.shape[0] // 2
    chosen = lax.broadcasted_iota(jnp.int32, (slots, PATCH), 0) == places[...]
    placed = dot(chosen.astype(BF), rows)
    pairs_ref[pl.ds(0, slots, 2), :] = placed[:, :LANES]
    pairs_ref[pl.ds(1, slots, 2), :] = placed[:, LANES:]
    packed_ref[...] = pairs_ref[...].astype(BF)


def unpack(arrived, places, pairs_ref):
    slots = arrived.shape[0] // 2
    pairs_ref[...] = arrived[...].astype(F32)
    placed = jnp.concatenate(
        [pairs_ref[pl.ds(0, slots, 2), :], pairs_ref[pl.ds(1, slots, 2), :]], axis=1
    ).astype(BF)
    columns = lax.broadcasted_iota(jnp.int32, (PATCH, slots), 1)
    return dot((columns == as_column(places[...])).astype(BF), placed).astype(BF)


def first_kernel(w, outs, scratch):
    packed_ref = outs[0]
    pairs_ref, sems, kept_sems = scratch[-3:]
    s = Scratch(
        ("value_t", "bias", "weights", "query_t", "heads_t", "inverse_sum", "key_rows",
         "value_rows", "middle_rows", "depart"),
        scratch[:-3],
    )
    started = []

    def keep(place, ref):
        copy = pltpu.make_async_copy(ref, outs[place], kept_sems.at[place - 1])
        copy.start()
        started.append(copy)

    def kept_copy(head):
        return pltpu.make_async_copy(s.weights.at[head], outs[7].at[head], sems.at[head])

    live = own_live(w.counts[lax.axis_index("patch")])
    x = w.rows[...].reshape(PATCH, WIDTH)
    key, value, middle = forward(x, live, w, s, lambda head: kept_copy(head).start())
    s.key_rows[...] = key
    s.value_rows[...] = value
    s.middle_rows[...] = middle
    for place, ref in enumerate(
        (s.key_rows, s.value_rows, s.middle_rows, s.query_t, s.heads_t, s.inverse_sum), 1
    ):
        keep(place, ref)
    _, _, _, pre = feed_forward(middle, w.up[...], w.gain_feed)
    block_out = (middle.astype(F32) + dot(gelu(pre).astype(BF), w.down[...])).astype(BF)
    targets = w.to_hilbert[...]
    s.depart[...] = places_of(targets, lax.broadcasted_iota(jnp.int32, targets.shape, 1))
    keep(8, s.depart)
    pack(block_out, s.depart, pairs_ref, packed_ref)

    for head in range(HEADS):
        kept_copy(head).wait()
    for copy in started:
        copy.wait()


def second_kernel(w, outs, scratch):
    out_ref, keep_ref, give_ref, packed_ref = outs
    s = Scratch(SCRATCH, scratch[:-2])
    rows_ref, pairs_ref = scratch[-2:]
    part = lax.axis_index("mp")
    core = lax.rem(lax.axis_index("patch"), 2)
    sources = w.from_hilbert[...]
    arrive = places_of(sources, sources)
    live = moved_live(sources, w.counts_row[...])
    x = unpack(w.arrived, arrive, pairs_ref)
    key, value, middle = forward(x, live, w, s)
    own = pl.ds(pl.multiple_of(part * (PATCH // 4), PATCH // 4), PATCH // 4)
    rows_ref[...] = middle
    middle_part = rows_ref[own, :]
    _, _, _, pre = feed_forward(middle_part, w.up[...], w.gain_feed)
    out_ref[...] = (
        middle_part.astype(F32) + dot(gelu(pre).astype(BF), w.down[...])
    ).astype(BF)
    cotangent = w.cotangent[...].reshape(PATCH, WIDTH)
    grad_in = backward(
        part, core, cotangent, x, middle, key, value, w, s, (keep_ref, give_ref), True
    )
    pack(grad_in, arrive, pairs_ref, packed_ref)


def last_kernel(w, outs, scratch):
    s = Scratch([name for name, _, _ in BACKWARD_SCRATCH], scratch[:-4], w)
    halves, pairs_ref, chunks_ref = scratch[-4:-2], scratch[-2], scratch[-1]
    w.start_rest()
    grad_rows = unpack(w.arrived, w.depart, pairs_ref)
    middle = w.middle[...]
    backward(
        lax.axis_index("mp"), lax.rem(lax.axis_index("patch"), 2), grad_rows, w.rows, middle,
        w.key_rows, w.value_rows, w, s, halves, False,
    )
    for out_ref, half, second in zip(outs, halves, (w.second_keep, w.second_give), strict=True):
        second = second[...].astype(F32)
        gains = jnp.concatenate(
            [half[WEIGHT_ROWS : WEIGHT_ROWS + 2, :], second[WEIGHT_ROWS : WEIGHT_ROWS + 2, :]],
            axis=0,
        )
        chips = out_ref.shape[0] // CHUNK_ROWS
        share = CHUNK_ROWS - GAIN_ROWS
        for chip in range(chips):
            block, first = divmod(chip * share, WEIGHT_ROWS)
            source = second if block else half
            there = chip * CHUNK_ROWS
            chunks_ref[there : there + share, :] = source[first : first + share, :]
            chunks_ref[there + share : there + CHUNK_ROWS, :] = gains
        out_ref[...] = chunks_ref[...].astype(BF)


def finish_kernel(w, outs, scratch):
    mixer_ref, query_ref, key_ref, value_ref, out_ref, feed_ref, up_ref, down_ref = outs
    own_ref, other_ref = w.own, w.other
    core = lax.rem(lax.axis_index("patch"), 2)
    own_rows, other_rows = own_ref[...].astype(F32), other_ref[...].astype(F32)

    def join(own, other):
        low = jnp.where(core == 0, own, other)
        return jnp.concatenate([low, jnp.where(core == 0, other, own)], axis=1)

    last = slice(2 * WEIGHT_ROWS, 2 * WEIGHT_ROWS + GAIN_ROWS)
    gains = join(own_rows[last, :], other_rows[last, :])
    for block in range(2):

        def rows(first, size):
            there = slice(WEIGHT_ROWS * block + first, WEIGHT_ROWS * block + first + size)
            return join(own_rows[there, :], other_rows[there, :])

        for place, ref in enumerate((query_ref, key_ref, value_ref, out_ref)):
            ref[block] = rows(64 * place, 64)
        for piece in range(4):
            up_ref[block, :, WIDTH * piece : WIDTH * (piece + 1)] = rows(256 + 64 * piece, 64)
        down_ref[block] = rows(512, 256)
        mixer_ref[block : block + 1, :] = gains[2 * block : 2 * block + 1, :]
        feed_ref[block : block + 1, :] = gains[2 * block + 1 : 2 * block + 2, :]


def whole(array):
    zeros = (0,) * len(array.shape)
    return pl.BlockSpec(array.shape, lambda step: zeros)


HBM = pl.BlockSpec(memory_space=pltpu.HBM)


def part_shape(shape, part):
    kept = [
        (place.size,) if isinstance(place, pl.Slice) else () if isinstance(place, int) else (size,)
        for size, place in zip(shape, part or ())
    ]
    return sum(kept, ()) + shape[len(kept) :]


def call(kernel, inputs, weights, block, early, outputs, scratch, name):
    inputs = [(name, array, part) for name, array, part in inputs]
    inputs += [
        (weight, array, None if weight in GAINS else (block,))
        for weight, array in zip(WEIGHTS, weights)
    ]
    inputs.sort(key=lambda entry: early.index(entry[0]) if entry[0] in early else len(early))
    names = [name for name, _, _ in inputs]
    parts = [part for _, _, part in inputs]
    arrays = [array for _, array, _ in inputs]
    shapes = [
        jax.ShapeDtypeStruct(part_shape(array.shape, part), array.dtype)
        for array, part in zip(arrays, parts)
    ]
    buffers = [
        pltpu.SMEM(shape.shape, shape.dtype)
        if name == "counts"
        else pltpu.VMEM(shape.shape, shape.dtype)
        for name, shape in zip(names, shapes)
    ]
    first_out, first_scratch = len(arrays), len(arrays) + len(outputs)
    first_buffer = first_scratch + len(scratch)

    def whole_kernel(*refs):
        sources = [
            ref if part is None else ref.at[part] for ref, part in zip(refs[:first_out], parts)
        ]
        taken = Inputs(names, sources, refs[first_buffer:-1], refs[-1], block, len(early))
        kernel(taken, refs[first_out:first_scratch], refs[first_scratch:first_buffer])

    return pl.pallas_call(
        whole_kernel,
        grid=(1,),
        out_shape=[shape for shape, _ in outputs],
        in_specs=[HBM] * len(arrays),
        out_specs=[spec or whole(shape) for shape, spec in outputs],
        scratch_shapes=[*scratch, *buffers, pltpu.SemaphoreType.DMA((len(arrays),))],
        compiler_params=pltpu.CompilerParams(
            vmem_limit_bytes=VMEM_BYTES if weights else VMEM_BYTES // 4
        ),
        name=name,
    )(*arrays)


def vmem(*names):
    return [pltpu.VMEM(SCRATCH[name][0], SCRATCH[name][1]) for name in names]


def first_call(counts, gathered, to_hilbert, weights, buffer_rows):
    rows = jax.ShapeDtypeStruct((PATCH, WIDTH), BF)
    turned = jax.ShapeDtypeStruct((WIDTH, PATCH), BF)
    return call(
        first_kernel,
        [("rows", gathered, (slice(None), 0)), ("counts", counts, None), ("to_hilbert", to_hilbert, None)],
        weights,
        0,
        ("rows", "gain_mixer", "query", "key", "value", "counts"),
        [(jax.ShapeDtypeStruct((buffer_rows, LANES), BF), None)]
        + [(rows, HBM)] * 3
        + [(turned, HBM)] * 2
        + [
            (jax.ShapeDtypeStruct((HEADS, 1, PATCH), F32), HBM),
            (jax.ShapeDtypeStruct((HEADS, PATCH, PATCH), BF), HBM),
            (jax.ShapeDtypeStruct((1, PATCH), jnp.int32), HBM),
        ],
        vmem("value_t", "bias", "weights", "query_t", "heads_t", "inverse_sum")
        + [pltpu.VMEM((PATCH, WIDTH), BF)] * 3
        + [pltpu.VMEM((1, PATCH), jnp.int32)]
        + [pltpu.VMEM((buffer_rows, LANES), F32)]
        + [pltpu.SemaphoreType.DMA((HEADS,)), pltpu.SemaphoreType.DMA((8,))],
        "first_block",
    )


def second_call(arrived, from_hilbert, counts, gathered, weights):
    half = jax.ShapeDtypeStruct((HALF_ROWS, LANES), BF)
    return call(
        second_kernel,
        [
            ("from_hilbert", from_hilbert, None), ("counts_row", counts, None),
            ("arrived", arrived, None),
            ("cotangent", gathered, (slice(None), 1)),
        ],
        weights,
        1,
        ("from_hilbert", "counts_row", "arrived", "gain_mixer", "query", "key", "value"),
        [
            (jax.ShapeDtypeStruct((PATCH // 4, WIDTH), BF), None), (half, None), (half, None),
            (jax.ShapeDtypeStruct(arrived.shape, BF), None),
        ],
        vmem(*SCRATCH) + [pltpu.VMEM((PATCH, WIDTH), BF), pltpu.VMEM(arrived.shape, F32)],
        "second_block",
    )


def last_call(arrived, gathered, kept, second, weights, chips):
    key, value, middle, query_t, heads_t, inverse, attention, depart = kept
    terms = jax.ShapeDtypeStruct((chips * CHUNK_ROWS, LANES), BF)
    return call(
        last_kernel,
        [
            ("depart", depart, None), ("arrived", arrived, None), ("middle", middle, None),
            ("heads_t", heads_t, None), ("rows", gathered, (slice(None), 0)),
            ("key_rows", key, None), ("value_rows", value, None), ("query_t", query_t, None),
            ("inverse_sum", inverse, None), ("second_keep", second[0], None),
            ("second_give", second[1], None),
        ]
        + [
            (f"weights{piece}", attention, (pl.ds(piece * HEADS // PIECES, HEADS // PIECES),))
            for piece in range(PIECES)
        ],
        weights,
        0,
        ("depart", "arrived", "middle", "gain_feed", "up", "down"),
        [(terms, None), (terms, None)],
        vmem(*[name for name, _, _ in BACKWARD_SCRATCH])
        + [pltpu.VMEM((HALF_ROWS, LANES), F32)] * 2
        + [pltpu.VMEM(arrived.shape, F32), pltpu.VMEM(terms.shape, F32)],
        "first_block_back",
    )


def finish_call(own, other):
    gain = jax.ShapeDtypeStruct((2, WIDTH), F32)
    small = jax.ShapeDtypeStruct((2, WIDTH // 4, WIDTH), F32)
    up = jax.ShapeDtypeStruct((2, WIDTH // 4, HIDDEN), F32)
    down = jax.ShapeDtypeStruct((2, HIDDEN // 4, WIDTH), F32)
    return call(
        finish_kernel,
        [("own", own, None), ("other", other, None)],
        (),
        0,
        ("own", "other"),
        [(shape, None) for shape in (gain, small, small, small, small, gain, up, down)],
        [],
        "finish",
    )


def exchange_rows(buffer):
    peers = lax.axis_size("patch")
    shaped = buffer.reshape(peers, buffer.shape[0] // (2 * peers), 2, LANES)
    return exchange(shaped).reshape(buffer.shape)


def exchange(buffer, groups=None):
    return lax.all_to_all(
        buffer, "patch", split_axis=0, concat_axis=0, tiled=True, axis_index_groups=groups
    )


def swap_cores(half, peer_count):
    return lax.ppermute(half, "patch", [(i, i ^ 1) for i in range(peer_count)])


def body(
    points,
    patch_counts,
    to_hilbert,
    from_hilbert,
    cotangent,
    gain_mixer,
    query_weight,
    key_weight,
    value_weight,
    out_weight,
    gain_feed,
    up_weight,
    down_weight,
):
    peer_count = lax.axis_size("patch")
    buffer_rows = 2 * peer_count * SLOTS
    weights = (
        gain_mixer,
        query_weight,
        key_weight,
        value_weight,
        out_weight,
        gain_feed,
        up_weight,
        down_weight,
    )
    pair = jnp.stack([points, cotangent])
    pair = jnp.broadcast_to(pair[None], (lax.axis_size("mp"),) + pair.shape)
    gathered = lax.all_to_all(pair, "mp", split_axis=0, concat_axis=0, tiled=True)
    sent, *kept = first_call(
        patch_counts, gathered, to_hilbert[None, :], weights, buffer_rows
    )
    arrived = exchange_rows(sent)
    hilbert_out, second_keep, second_give, grad_sent = second_call(
        arrived, from_hilbert[None, :], patch_counts[None, :], gathered, weights
    )
    grad_arrived = exchange_rows(grad_sent)
    chips = peer_count // 2
    keep, give = last_call(
        grad_arrived, gathered, kept, (second_keep, second_give), weights, chips,
    )
    taken = swap_cores(give, peer_count)
    terms = (keep.astype(F32) + taken.astype(F32)).astype(BF)
    groups = [[2 * chip + core for chip in range(chips)] for core in range(2)]
    arrived_terms = exchange(terms.reshape(chips, CHUNK_ROWS // 4, 4, LANES), groups)
    sums = jnp.sum(arrived_terms.astype(F32), axis=0).astype(BF).reshape(CHUNK_ROWS, LANES)
    share = CHUNK_ROWS - GAIN_ROWS
    spread = jnp.broadcast_to(sums[None, :share], (chips, share, LANES))
    own, sums = lax.optimization_barrier((exchange(spread, groups), sums))
    own = own.reshape(chips * share, LANES)
    own = jnp.concatenate([own, sums[share:], jnp.zeros((16 - GAIN_ROWS, LANES), BF)], axis=0)
    other = swap_cores(own, peer_count)
    return (hilbert_out, *finish_call(own, other))


def solution(mesh):
    split = P(("patch", "mp"), None)
    in_specs = (split, P(), P("patch"), P("patch"), split) + (P(),) * 8
    own_rows = P(None, "mp", None)
    out_specs = (split, P(), own_rows, own_rows, own_rows, own_rows, P(), own_rows, own_rows)
    return jax.shard_map(body, mesh=mesh, in_specs=in_specs, out_specs=out_specs, check_vma=False)
```

profile of v0, /device:TPU:1, one launch (start us, length us, event | category | flops | bytes accessed | tf_op | source)
XLA Modules:
  0.0 193.5 jit_solution(13950973224387948244)
XLA Ops:
  0.6 0.9 pad_maximum_fusion
  1.6 11.7 %all_to_all.25.refs_0_.refs_7_ = bf16[4,2,128,256]{3,2,1,0:T(8,128)(2,1)} all-to-all(bf16[4,2,128,256]{3,2,1,0:T(8,128)(2,1)S(1)} %broadcast_in_dim.28), channel_id=1, replica_groups=mesh['patch'=128,'mp'=4] {'mp'}, dimensions={0} | all-to-all | bytes 1048576 | tf_op jit(solution)/shard_map/all_to_all | solution.py:629
  13.3 10.9 %first_block.1 = (bf16[1536,128]{1,0:T(8,128)(2,1)}, bf16[512,256]{1,0:T(8,128)(2,1)}, bf16[512,256]{1,0:T(8,128)(2,1)}, bf16[512,256]{1,0:T(8,128)(2,1)}, bf16[...) custom-call(bf16[4,2,128,256]{3,2,1,0:T(8,128)(2,1)} %all_to_all.25., ...), custom_call_target="tpu_custom_call" | custom-call | tf_op jit(solution)/shard_map/first_block/pallas_call | solution.py:475
  24.2 38.4 %all_to_all.26 = bf16[128,6,2,128]{3,2,1,0:T(2,128)(2,1)} all-to-all(bf16[128,6,2,128]{3,2,1,0:T(2,128)(2,1)} %bitcast.16), channel_id=1, replica_groups=mesh['patch'=128,'mp'=4] {'patch'}, dimensions={0} | all-to-all | bytes 786432 | tf_op jit(solution)/shard_map/all_to_all | solution.py:591
  62.6 34.7 %second_block.1 = (bf16[128,256]{1,0:T(8,128)(2,1)}, bf16[784,128]{1,0:T(8,128)(2,1)}, bf16[784,128]{1,0:T(8,128)(2,1)}, bf16[1536,128]{1,0:T(8,128)(2,1)}) custom-call(s32[1,512]{1,0:T(1,128)} %bitcast.22, s32[1,128]{1,0:T(1,128)} %bitcast.23, bf16[1536,128]{1,0:T(8,128)(2,1)} %bitcast.14, f32[2,256]{1,0:T(2,128)} %refs_15_.1, ...), custom_call_target="tpu_custom_call" | custom-call | tf_op jit(solution)/shard_map/second_block/pallas_call | solution.py:475
  97.4 24.3 %all_to_all.27 = bf16[128,6,2,128]{3,2,1,0:T(2,128)(2,1)} all-to-all(bf16[128,6,2,128]{3,2,1,0:T(2,128)(2,1)} %bitcast.17), channel_id=1, replica_groups=mesh['patch'=128,'mp'=4] {'patch'}, dimensions={0} | all-to-all | bytes 786432 | tf_op jit(solution)/shard_map/all_to_all | solution.py:591
  121.7 15.4 %first_block_back.1 = (bf16[1792,128]{1,0:T(8,128)(2,1)}, bf16[1792,128]{1,0:T(8,128)(2,1)}) custom-call(s32[1,512]{1,0:T(1,128)} %get-tuple-element.36.refs_0_, bf16[1536,128]{1,0:T(8,128)(2,1)} %bitcast.15, bf16[512,256]{1,0:T(8,128)(2,1)} %get-tuple-element.38.refs_2_, f32[2,256]{1,0:T(2,128)} %refs_3_.5, bf16[2,256,1024]{2,1,0:T(8,128)(2,1)} %refs_4_.5, ...), custom_call_target="tpu_custom_call" | custom-call | tf_op jit(solution)/shard_map/first_block_back/pallas_call | solution.py:475
  137.1 2.1 %collective-permute-start = (bf16[1792,128]{1,0:T(8,128)(2,1)}, bf16[1792,128]{1,0:T(8,128)(2,1)S(1)}, u32[]{:S(2)}, u32[]{:S(2)}) collective-permute-start(bf16[1792,128]{1,0:T(8,128)(2,1)} %get-tuple-element.48), channel_id=1, source_target_pairs={{0,4},{4,0},{8,12},{12,8},{16,20},{20,16},{24,28},{28,24},{32,36},... | collective-permute-start | bytes 1376264 | tf_op jit(solution)/shard_map/ppermute | solution.py:597
  139.2 1.8 collective-permute-done
  141.0 1.1 add_convert_fusion
  142.2 20.6 %all_to_all.28 = bf16[64,7,4,128]{3,2,1,0:T(4,128)(2,1)S(1)} all-to-all(bf16[64,7,4,128]{3,2,1,0:T(4,128)(2,1)S(1)} %bitcast.12), channel_id=1, replica_groups={{0,8,16,24,32,40,48,56,64,72,80,88,96,104,112,120,128,136,144,152,160,1..., dimensions={0} | all-to-all | bytes 917504 | tf_op jit(solution)/shard_map/all_to_all | solution.py:591
  162.7 0.2 reduce_sum.12
  163.0 0.8 broadcast_in_dim.31
  163.8 6.2 %all-to-all-start.4 = ((bf16[64,24,128]{2,1,0:T(8,128)(2,1)}), bf16[64,24,128]{2,1,0:T(8,128)(2,1)S(1)}, u32[]{:S(2)}, u32[]{:S(2)}) async-start(bf16[64,24,128]{2,1,0:T(8,128)(2,1)} %broadcast_in_dim.31), calls=%async_computation.4 | async-start | bytes 786432 | tf_op jit(solution)/shard_map/all_to_all | solution.py:591
  170.0 14.0 %all-to-all-done.4 = bf16[64,24,128]{2,1,0:T(8,128)(2,1)S(1)} async-done(((bf16[64,24,128]{2,1,0:T(8,128)(2,1)}), bf16[64,24,128]{2,1,0:T(8,128)(2,1)S(1)}, u32[]{:S(2)}, u32[]{:S(2)}) %all-to-all-start.4) | async-done | bytes 393248 | tf_op jit(solution)/shard_map/all_to_all | solution.py:591
  184.0 0.3 concatenate.3.refs_0_
  184.3 6.1 %collective-permute-start.1 = (bf16[1552,128]{1,0:T(8,128)(2,1)S(1)}, bf16[1552,128]{1,0:T(8,128)(2,1)S(1)}, u32[]{:S(2)}, u32[]{:S(2)}) collective-permute-start(bf16[1552,128]{1,0:T(8,128)(2,1)S(1)} %concatenate.3.refs_0_), channel_id=1, source_target_pairs={{0,4},{4,0},{8,12},{12,8},{16,20},{20,16},{24,28},{28,24},{32,36},... | collective-permute-start | bytes 1191944 | tf_op jit(solution)/shard_map/ppermute | solution.py:597
  190.4 1.3 collective-permute-done.1.refs_1_
  191.8 1.6 finish.1
  (5 shorter events, 0.1 us)
Async XLA Ops:
  137.1 3.9 %collective-permute-start = (bf16[1792,128]{1,0:T(8,128)(2,1)}, bf16[1792,128]{1,0:T(8,128)(2,1)S(1)}, u32[]{:S(2)}, u32[]{:S(2)}) collective-permute-start(bf16[1792,128]{1,0:T(8,128)(2,1)} %get-tuple-element.48), channel_id=1, source_target_pairs={{0,4},{4,0},{8,12},{12,8},{16,20},{20,16},{24,28},{28,24},{32,36},... | collective-permute-start | bytes 1376264 | tf_op jit(solution)/shard_map/ppermute | solution.py:597
  163.8 20.2 %all-to-all-start.4 = ((bf16[64,24,128]{2,1,0:T(8,128)(2,1)}), bf16[64,24,128]{2,1,0:T(8,128)(2,1)S(1)}, u32[]{:S(2)}, u32[]{:S(2)}) async-start(bf16[64,24,128]{2,1,0:T(8,128)(2,1)} %broadcast_in_dim.31), calls=%async_computation.4 | async-start | bytes 786432 | tf_op jit(solution)/shard_map/all_to_all | solution.py:591
  184.3 7.5 %collective-permute-start.1 = (bf16[1552,128]{1,0:T(8,128)(2,1)S(1)}, bf16[1552,128]{1,0:T(8,128)(2,1)S(1)}, u32[]{:S(2)}, u32[]{:S(2)}) collective-permute-start(bf16[1552,128]{1,0:T(8,128)(2,1)S(1)} %concatenate.3.refs_0_), channel_id=1, source_target_pairs={{0,4},{4,0},{8,12},{12,8},{16,20},{20,16},{24,28},{28,24},{32,36},... | collective-permute-start | bytes 1191944 | tf_op jit(solution)/shard_map/ppermute | solution.py:597
where the time goes:
time: 194 us
  blocking collectives  95 us (49%)
  Pallas kernels  62.7 us (32%)
  waiting for transfers between devices  17.1 us (9%)
  starting transfers between devices  14.4 us (7%)
  other arithmetic  2.24 us (1%)
    all_to_all x3, blocking collectives, exchange(): lax.all_to_all(buffer, 'patch', split_axis=0, concat_axis=0, tiled=True,...  83.3 us
    pallas_call x4, Pallas kernels, call(): pl.pallas_call(whole_kernel, grid=(1,), out_shape=[shape for shape, _ in...  62.7 us
    all_to_all x1, waiting for transfers between devices, exchange(): lax.all_to_all(buffer, 'patch', split_axis=0, concat_axis=0, tiled=True,...  14 us
    all_to_all x1, blocking collectives, body(): lax.all_to_all(pair, 'mp', split_axis=0, concat_axis=0, tiled=True)  11.7 us
    ppermute x2, starting transfers between devices, swap_cores(): return lax.ppermute(half, 'patch', [(i, i ^ 1) for i in range(peer_count)])  8.23 us
    all_to_all x1, starting transfers between devices, exchange(): lax.all_to_all(buffer, 'patch', split_axis=0, concat_axis=0, tiled=True,...  6.21 us
  transfers between devices with their start and end apart: 3, of which 3 were waited for; matrix products, arithmetic and copies ran while one was open for 0% of the time, Pallas kernels for 0%

commit v1 on v0

--- a/solution.py
+++ b/solution.py
@@ -442,7 +442,9 @@
     return sum(kept, ()) + shape[len(kept) :]
 
 
-def call(kernel, inputs, weights, block, early, outputs, scratch, name):
+def call(
+    kernel, inputs, weights, block, early, outputs, scratch, name, vmem_bytes=VMEM_BYTES
+):
     inputs = [(name, array, part) for name, array, part in inputs]
     inputs += [
         (weight, array, None if weight in GAINS else (block,))
@@ -480,7 +482,7 @@
         out_specs=[spec or whole(shape) for shape, spec in outputs],
         scratch_shapes=[*scratch, *buffers, pltpu.SemaphoreType.DMA((len(arrays),))],
         compiler_params=pltpu.CompilerParams(
-            vmem_limit_bytes=VMEM_BYTES if weights else VMEM_BYTES // 4
+            vmem_limit_bytes=vmem_bytes
         ),
         name=name,
     )(*arrays)
@@ -561,6 +563,7 @@
         + [pltpu.VMEM((HALF_ROWS, LANES), F32)] * 2
         + [pltpu.VMEM(arrived.shape, F32), pltpu.VMEM(terms.shape, F32)],
         "first_block_back",
+        40 * 1024 * 1024,
     )
 
 
@@ -578,6 +581,7 @@
         [(shape, None) for shape in (gain, small, small, small, small, gain, up, down)],
         [],
         "finish",
+        VMEM_BYTES // 4,
     )
 
 
@@ -646,9 +650,9 @@
     sums = jnp.sum(arrived_terms.astype(F32), axis=0).astype(BF).reshape(CHUNK_ROWS, LANES)
     share = CHUNK_ROWS - GAIN_ROWS
     spread = jnp.broadcast_to(sums[None, :share], (chips, share, LANES))
-    own, sums = lax.optimization_barrier((exchange(spread, groups), sums))
-    own = own.reshape(chips * share, LANES)
-    own = jnp.concatenate([own, sums[share:], jnp.zeros((16 - GAIN_ROWS, LANES), BF)], axis=0)
+    own = exchange(spread, groups).reshape(chips * share, LANES)
+    gain_rows = sums[share:] + own[:GAIN_ROWS] * 0
+    own = jnp.concatenate([own, gain_rows, jnp.zeros((16 - GAIN_ROWS, LANES), BF)], axis=0)
     other = swap_cores(own, peer_count)
     return (hilbert_out, *finish_call(own, other))
 

time: 194 us -> 200 us (1.031)
  blocking collectives: 95 us -> 114 us
  waiting for transfers between devices: 17.1 us -> 2.95 us
  local copies, waits for them, and re-layouts: 1.14 us -> 8.48 us
  starting transfers between devices: 14.4 us -> 8.23 us
    all_to_all x3 -> x4, blocking collectives: 83.3 us -> 103 us  [exchange(): lax.all_to_all(buffer, 'patch', split_axis=0, concat_axis=0, tiled=True,...]
    all_to_all x1 -> x0, waiting for transfers between devices: 14 us -> none  [exchange(): lax.all_to_all(buffer, 'patch', split_axis=0, concat_axis=0, tiled=True,...]
    unnamed x0 -> x36, local copies, waits for them, and re-layouts: none -> 8.09 us
    all_to_all x1 -> x0, starting transfers between devices: 6.21 us -> none  [exchange(): lax.all_to_all(buffer, 'patch', split_axis=0, concat_axis=0, tiled=True,...]
  transfers between devices with their start and end apart: 3 -> 2, of which waited for: 3 -> 2; matrix products, arithmetic and copies ran while one was open for 0% -> 0% of each run, Pallas kernels for 0% -> 0%
where the time goes in v1:
time: 200 us; the launch traced here: 199 us
  blocking collectives  114 us (57%)
  Pallas kernels  62.7 us (31%)
  local copies, waits for them, and re-layouts  8.48 us (4%)
  starting transfers between devices  8.23 us (4%)
  waiting for transfers between devices  2.95 us (1%)
    all_to_all x4, blocking collectives, exchange(): lax.all_to_all(buffer, 'patch', split_axis=0, concat_axis=0, tiled=True,...  103 us
    pallas_call x4, Pallas kernels, call(): pl.pallas_call(whole_kernel, grid=(1,), out_shape=[shape for shape, _ in...  62.7 us
    all_to_all x1, blocking collectives, body(): lax.all_to_all(pair, 'mp', split_axis=0, concat_axis=0, tiled=True)  11.7 us
    ppermute x2, starting transfers between devices, swap_cores(): return lax.ppermute(half, 'patch', [(i, i ^ 1) for i in range(peer_count)])  8.23 us
    unnamed x36, local copies, waits for them, and re-layouts  8.09 us
  transfers between devices with their start and end apart: 2, of which 2 were waited for; matrix products, arithmetic and copies ran while one was open for 0% of the time, Pallas kernels for 0%

profile of v1, /device:TPU:1, one launch (start us, length us, event | category | flops | bytes accessed | tf_op | source)
XLA Modules:
  0.0 199.1 jit_solution(4692677506096725925)
XLA Ops:
  0.7 1.0 pad_maximum_fusion
  1.8 11.7 %all_to_all.25.refs_0_.refs_7_ = bf16[4,2,128,256]{3,2,1,0:T(8,128)(2,1)} all-to-all(bf16[4,2,128,256]{3,2,1,0:T(8,128)(2,1)S(1)} %broadcast_in_dim.28), channel_id=1, replica_groups=mesh['patch'=128,'mp'=4] {'mp'}, dimensions={0} | all-to-all | bytes 1048576 | tf_op jit(solution)/shard_map/all_to_all | solution.py:633
  13.5 11.0 %first_block.1 = (bf16[1536,128]{1,0:T(8,128)(2,1)}, bf16[512,256]{1,0:T(8,128)(2,1)}, bf16[512,256]{1,0:T(8,128)(2,1)}, bf16[512,256]{1,0:T(8,128)(2,1)}, bf16[...) custom-call(bf16[4,2,128,256]{3,2,1,0:T(8,128)(2,1)} %all_to_all.25., ...), custom_call_target="tpu_custom_call" | custom-call | tf_op jit(solution)/shard_map/first_block/pallas_call | solution.py:477
  24.5 38.4 %all_to_all.26 = bf16[128,6,2,128]{3,2,1,0:T(2,128)(2,1)} all-to-all(bf16[128,6,2,128]{3,2,1,0:T(2,128)(2,1)} %bitcast.21), channel_id=1, replica_groups=mesh['patch'=128,'mp'=4] {'patch'}, dimensions={0} | all-to-all | bytes 786432 | tf_op jit(solution)/shard_map/all_to_all | solution.py:595
  63.0 34.9 %second_block.1 = (bf16[128,256]{1,0:T(8,128)(2,1)}, bf16[784,128]{1,0:T(8,128)(2,1)}, bf16[784,128]{1,0:T(8,128)(2,1)}, bf16[1536,128]{1,0:T(8,128)(2,1)}) custom-call(s32[1,512]{1,0:T(1,128)} %bitcast.27, s32[1,128]{1,0:T(1,128)} %bitcast.28, bf16[1536,128]{1,0:T(8,128)(2,1)} %bitcast.20, f32[2,256]{1,0:T(2,128)} %refs_15_.1, ...), custom_call_target="tpu_custom_call" | custom-call | tf_op jit(solution)/shard_map/second_block/pallas_call | solution.py:477
  97.9 23.6 %all_to_all.27 = bf16[128,6,2,128]{3,2,1,0:T(2,128)(2,1)S(1)} all-to-all(bf16[128,6,2,128]{3,2,1,0:T(2,128)(2,1)} %bitcast.22), channel_id=1, replica_groups=mesh['patch'=128,'mp'=4] {'patch'}, dimensions={0} | all-to-all | bytes 786432 | tf_op jit(solution)/shard_map/all_to_all | solution.py:595
  121.6 0.9 copy-done.7
  122.5 0.9 copy-done.8
  123.5 0.9 copy-done.9
  124.4 0.9 copy-done.10
  125.4 0.9 copy-done.11
  126.3 0.9 copy-done.12
  127.3 0.9 copy-done.13
  128.2 0.8 copy-done.14
  128.9 0.7 copy-done.17
  129.6 15.2 %first_block_back.1 = (bf16[1792,128]{1,0:T(8,128)(2,1)S(1)}, bf16[1792,128]{1,0:T(8,128)(2,1)S(1)}) custom-call(s32[1,512]{1,0:T(1,128)S(1)} %copy-done.17, bf16[1536,128]{1,0:T(8,128)(2,1)S(1)} %bitcast.16, bf16[512,256]{1,0:T(8,128)(2,1)S(1)} %copy-done.9, f32[2,256]{1,0:T(2,128)S(1)} %copy-done.16, bf16[2,256,1024]{2,1,0:T(8,128)(2,1)S(1)} %copy-done, ...), custom_call_target="tpu_custom_call" | custom-call | tf_op jit(solution)/shard_map/first_block_back/pallas_call | solution.py:477
  144.8 2.1 %collective-permute-start = (bf16[1792,128]{1,0:T(8,128)(2,1)S(1)}, bf16[1792,128]{1,0:T(8,128)(2,1)S(1)}, u32[]{:S(2)}, u32[]{:S(2)}) collective-permute-start(bf16[1792,128]{1,0:T(8,128)(2,1)S(1)} %get-tuple-element.46), channel_id=1, source_target_pairs={{0,4},{4,0},{8,12},{12,8},{16,20},{20,16},{24,28},{28,24},{32,36},... | collective-permute-start | bytes 1376264 | tf_op jit(solution)/shard_map/ppermute | solution.py:601
  146.9 1.6 collective-permute-done
  148.6 20.6 %all_to_all.28 = bf16[64,7,4,128]{3,2,1,0:T(4,128)(2,1)S(1)} all-to-all(bf16[64,7,4,128]{3,2,1,0:T(4,128)(2,1)S(1)} %bitcast.17), channel_id=1, replica_groups={{0,8,16,24,32,40,48,56,64,72,80,88,96,104,112,120,128,136,144,152,160,1..., dimensions={0} | all-to-all | bytes 917504 | tf_op jit(solution)/shard_map/all_to_all | solution.py:595
  169.5 20.0 %all_to_all.29 = bf16[64,24,128]{2,1,0:T(8,128)(2,1)S(1)} all-to-all(bf16[64,24,128]{2,1,0:T(8,128)(2,1)S(1)} %broadcast_in_dim.31), channel_id=1, replica_groups={{0,8,16,24,32,40,48,56,64,72,80,88,96,104,112,120,128,136,144,152,160,1..., dimensions={0} | all-to-all | bytes 786432 | tf_op jit(solution)/shard_map/all_to_all | solution.py:595
  189.5 0.3 concatenate.3.refs_0_
  189.8 6.1 %collective-permute-start.1 = (bf16[1552,128]{1,0:T(8,128)(2,1)S(1)}, bf16[1552,128]{1,0:T(8,128)(2,1)S(1)}, u32[]{:S(2)}, u32[]{:S(2)}) collective-permute-start(bf16[1552,128]{1,0:T(8,128)(2,1)S(1)} %concatenate.3.refs_0_), channel_id=1, source_target_pairs={{0,4},{4,0},{8,12},{12,8},{16,20},{20,16},{24,28},{28,24},{32,36},... | collective-permute-start | bytes 1191944 | tf_op jit(solution)/shard_map/ppermute | solution.py:601
  196.0 1.3 collective-permute-done.1.refs_1_
  197.3 1.6 finish.1
  (34 shorter events, 0.5 us)
Async XLA Ops:
  0.6 120.9 %copy-start.15 = (f32[2,256]{1,0:T(2,128)S(1)}, f32[2,256]{1,0:T(2,128)}, u32[]{:S(2)}) copy-start(f32[2,256]{1,0:T(2,128)} %refs_15_.1) | copy-start | bytes 6148
  0.7 120.8 %copy-start.3 = (bf16[2,256,256]{2,1,0:T(8,128)(2,1)S(1)}, bf16[2,256,256]{2,1,0:T(8,128)(2,1)}, u32[]{:S(2)}) copy-start(bf16[2,256,256]{2,1,0:T(8,128)(2,1)} %refs_16_.1) | copy-start | bytes 786436
  0.7 120.8 %copy-start.4 = (bf16[2,256,256]{2,1,0:T(8,128)(2,1)S(1)}, bf16[2,256,256]{2,1,0:T(8,128)(2,1)}, u32[]{:S(2)}) copy-start(bf16[2,256,256]{2,1,0:T(8,128)(2,1)} %refs_17_.1) | copy-start | bytes 786436
  0.7 120.8 %copy-start.5 = (bf16[2,256,256]{2,1,0:T(8,128)(2,1)S(1)}, bf16[2,256,256]{2,1,0:T(8,128)(2,1)}, u32[]{:S(2)}) copy-start(bf16[2,256,256]{2,1,0:T(8,128)(2,1)} %refs_18_.1) | copy-start | bytes 786436
  0.7 120.8 %copy-start.6 = (bf16[2,256,256]{2,1,0:T(8,128)(2,1)S(1)}, bf16[2,256,256]{2,1,0:T(8,128)(2,1)}, u32[]{:S(2)}) copy-start(bf16[2,256,256]{2,1,0:T(8,128)(2,1)} %refs_19_.1) | copy-start | bytes 786436
  0.7 120.8 %copy-start.16 = (f32[2,256]{1,0:T(2,128)S(1)}, f32[2,256]{1,0:T(2,128)}, u32[]{:S(2)}) copy-start(f32[2,256]{1,0:T(2,128)} %refs_3_.5) | copy-start | bytes 6148
  0.7 120.8 %copy-start = (bf16[2,256,1024]{2,1,0:T(8,128)(2,1)S(1)}, bf16[2,256,1024]{2,1,0:T(8,128)(2,1)}, u32[]{:S(2)}) copy-start(bf16[2,256,1024]{2,1,0:T(8,128)(2,1)} %refs_4_.5) | copy-start | bytes 3145732
  0.7 120.8 %copy-start.1 = (bf16[2,1024,256]{2,1,0:T(8,128)(2,1)S(1)}, bf16[2,1024,256]{2,1,0:T(8,128)(2,1)}, u32[]{:S(2)}) copy-start(bf16[2,1024,256]{2,1,0:T(8,128)(2,1)} %refs_5_.5) | copy-start | bytes 3145732
  13.5 108.1 %copy-start.2 = (bf16[4,2,128,256]{3,2,1,0:T(8,128)(2,1)S(1)}, bf16[4,2,128,256]{3,2,1,0:T(8,128)(2,1)}, u32[]{:S(2)}) copy-start(bf16[4,2,128,256]{3,2,1,0:T(8,128)(2,1)} %all_to_all.25.refs_0_.refs_7_) | copy-start | bytes 1572868
  121.6 1.0 copy-start.7
  122.5 0.9 copy-start.8
  123.5 0.9 copy-start.9
  124.4 0.9 copy-start.10
  125.4 0.9 copy-start.11
  126.3 0.9 copy-start.12
  127.3 0.9 copy-start.13
  128.2 0.8 copy-start.14
  128.9 0.7 copy-start.17
  144.8 3.7 %collective-permute-start = (bf16[1792,128]{1,0:T(8,128)(2,1)S(1)}, bf16[1792,128]{1,0:T(8,128)(2,1)S(1)}, u32[]{:S(2)}, u32[]{:S(2)}) collective-permute-start(bf16[1792,128]{1,0:T(8,128)(2,1)S(1)} %get-tuple-element.46), channel_id=1, source_target_pairs={{0,4},{4,0},{8,12},{12,8},{16,20},{20,16},{24,28},{28,24},{32,36},... | collective-permute-start | bytes 1376264 | tf_op jit(solution)/shard_map/ppermute | solution.py:601
  189.8 7.5 %collective-permute-start.1 = (bf16[1552,128]{1,0:T(8,128)(2,1)S(1)}, bf16[1552,128]{1,0:T(8,128)(2,1)S(1)}, u32[]{:S(2)}, u32[]{:S(2)}) collective-permute-start(bf16[1552,128]{1,0:T(8,128)(2,1)S(1)} %concatenate.3.refs_0_), channel_id=1, source_target_pairs={{0,4},{4,0},{8,12},{12,8},{16,20},{20,16},{24,28},{28,24},{32,36},... | collective-permute-start | bytes 1191944 | tf_op jit(solution)/shard_map/ppermute | solution.py:601
